TPU v7x, 32 devices: a whole 2x2x4 slice. The times are simulated.
32 devices in a mesh: rows: 4 (over y, x), pairs: 8 (over z, core).
Axes of the slice: x: 2, y: 2, z: 4, core: 2. Of those that a mesh axis runs over, the one named last changes fastest.
Arguments:
- unit_rows: float32 [4, 8, 384, 4096], P('rows', 'pairs'), may hold values from -6 to 6
- unit_counts: int32 [4, 8], P('rows'), may hold values from 1 to 384, 1024 in all within a row
- seating: int32 [16], replicated, may hold values from 0 to 15, each once
- channel_scale: float32 [4096], replicated, may hold values from 0.25 to 4
Outputs:
- rotated: float32 [4096, 4096], P('rows', 'pairs')
Inputs may be any that keep to these rules, and one draw needn't show every extreme that they name: `unit_counts`: each row of 8 counts sums to 1024, and in each row the largest is exactly 384. `seating`: each block once.
All inputs are finite; a program needn't handle non-finite values.
Results may differ from a plain program's by a relative error of at most 0.0001.
Values sent between devices are 32-bit elements; how exact they have to be, the bound alone decides.
A program may use at most 128 MiB of HBM per device.

v0:
```python
import jax
import jax.numpy as jnp
from jax import lax
from jax.sharding import PartitionSpec as P

ROWS_DEV = 1024
BLOCK = 256
ROUNDS = 2


epsilon = 1e-06


def passed_along(array, axis, by):
    length = lax.axis_size(axis)
    pairs = [(i, i + by) for i in range(length) if 0 <= i + by < length]
    return lax.ppermute(array, axis, pairs)


def rotate(panels):
    partial_gram = lax.dot_general(
        panels,
        panels,
        (((0,), (0,)), ((), ())),
        precision=lax.Precision.HIGHEST,
        preferred_element_type=jnp.float32,
    )
    gram_full = lax.psum(partial_gram, "rows")
    diag_terms = jnp.diagonal(gram_full)
    skew_part = (
        gram_full
        * (diag_terms[None, :] - diag_terms[:, None])
        / (2.0 * (diag_terms[:, None] ** 2 + diag_terms[None, :] ** 2) + epsilon)
    )
    skew_square = jnp.dot(skew_part, skew_part, precision=lax.Precision.HIGHEST)
    identity = jnp.eye(skew_part.shape[0], dtype=jnp.float32)
    numerator = identity + skew_part + 0.25 * skew_square
    sym_part = identity - 0.25 * skew_square
    factor = jnp.linalg.cholesky(sym_part)
    transposed = jax.scipy.linalg.cho_solve((factor, True), numerator.T)
    return jnp.dot(panels, transposed.T, precision=lax.Precision.HIGHEST)


def advance(panels):
    half_width = panels.shape[1] // 2
    upper = panels[:, :half_width]
    lower = panels[:, half_width:]
    pair_index = lax.axis_index("pairs")
    last_pair = lax.axis_size("pairs") - 1
    upward = jnp.where(pair_index == 0, lower, upper)
    came_up = passed_along(upward, "pairs", 1)
    came_down = passed_along(lower, "pairs", -1)
    new_upper = jnp.where(pair_index == 0, upper, came_up)
    new_lower = jnp.where(pair_index == last_pair, upper, came_down)
    return jnp.concatenate([new_upper, new_lower], axis=1)


def compact(panels, group_counts, capacity):
    unit_ends = jnp.cumsum(group_counts)
    target = lax.iota(jnp.int32, ROWS_DEV)
    passed = (target[:, None] >= unit_ends[None, :]).astype(jnp.int32)
    owner_unit = jnp.sum(passed, axis=1)
    owner_start = jnp.sum(passed * group_counts[None, :], axis=1)
    source = owner_unit * capacity + target - owner_start
    return jnp.take(panels, source, axis=0)


def local(unit_rows, unit_counts, seating, channel_scale):
    capacity = unit_rows.shape[2]
    columns = unit_rows.shape[3]
    group_counts = unit_counts[0]
    pair_index = lax.axis_index("pairs")
    slot_ids = lax.iota(jnp.int32, group_counts.shape[0])
    own_count = jnp.sum(jnp.where(slot_ids == pair_index, group_counts, 0))
    live_rows = (lax.iota(jnp.int32, capacity) < own_count)[:, None]
    scaled = jnp.where(live_rows, unit_rows[0, 0] * channel_scale[None, :], 0.0)
    seated = jnp.take(scaled.reshape(capacity, columns // BLOCK, BLOCK), seating, axis=1).reshape(
        capacity, columns
    )
    panels = lax.all_to_all(seated, "pairs", split_axis=1, concat_axis=0, tiled=True)
    current = panels
    for round_index in range(ROUNDS):
        current = rotate(current)
        if round_index + 1 < ROUNDS:
            current = advance(current)
    current = compact(current, group_counts, capacity)
    return current


def solution(mesh):
    return jax.shard_map(
        local,
        mesh=mesh,
        in_specs=(P("rows", "pairs", None, None), P("rows", None), P(), P()),
        out_specs=P("rows", "pairs"),
        check_vma=False,
    )
```

profile of v0, /device:TPU:16, one launch (start us, length us, event | category | flops | bytes accessed | tf_op | source)
XLA Modules:
  0.0 765.0 jit_solution(10047440830474087624)
XLA Ops:
  9.8 6.6 copy.36
  16.4 6.5 copy.37
  23.0 6.3 multiply_select_fusion
  29.3 6.4 gather_fusion
  35.7 6.5 copy.38
  42.2 6.6 copy.39
  49.0 3.6 broadcast_select_fusion
  52.6 140.9 %all_to_all.16 = f32[384,8,512]{2,0,1:T(8,128)S(1)} all-to-all(f32[384,8,512]{2,0,1:T(8,128)S(1)} %broadcast_select_fusion), channel_id=1, replica_groups=mesh['rows'=4,'pairs'=8] {'pairs'}, dimensions={1} | all-to-all | bytes 12582912 | tf_op jit(solution)/shard_map/all_to_all | solution.py:80
  193.6 2.7 copy-done.1
  196.2 11.4 %fusion.4 = f32[512,512]{0,1:T(8,128)} fusion(f32[384,8,512]{2,0,1:T(8,128)S(1)} %all_to_all.16), kind=kOutput, calls=%fused_computation.22 | convolution fusion | flops 9663676416 | bytes 7340032 | tf_op jit(solution)/shard_map/dot_general | solution.py:21
  207.8 54.2 %all-reduce.4.cloned.1.call-done = f32[512,512]{0,1:T(8,128)} async-done(((f32[512,512]{0,1:T(8,128)}), f32[512,512]{0,1:T(8,128)}) %all-reduce.4.cloned.1.call-update) | async-done | bytes 1048592 | tf_op jit(solution)/shard_map/psum | solution.py:28
  262.0 8.8 %gather_fusion.1 = f32[512]{0:T(512)S(1)} fusion(f32[512,512]{0,1:T(8,128)} %all-reduce.4.cloned.1.call-done, s32[512]{0:T(512)S(1)} %bitcast.140), kind=kCustom, calls=%fused_computation.1 | custom fusion | bytes 8192 | tf_op jit(solution)/shard_map/jit(diagonal)/cond/branch_0_fun/gather | solution.py:29
  270.8 4.1 convolution_multiply_fusion.1
  274.9 1.4 convert_subtract_fusion.1
  277.9 11.7 %cholesky.286 = f32[128,128]{1,0:T(8,128)S(1)} custom-call(f32[128,128]{1,0:T(8,128)S(1)} %cholesky.426), custom_call_target="Cholesky" | custom-call | tf_op jit(solution)/shard_map/jit(cholesky)/cholesky | solution.py:39
  289.6 9.8 %custom-call.33 = f32[1,128,128]{1,2,0:T(8,128)S(1)} custom-call(f32[1,128,128]{2,1,0:T(8,128)S(1)} %get-tuple-element.72), custom_call_target="InvertDiagBlocksLowerTriangular" | custom-call | tf_op jit(solution)/shard_map/jit(cholesky)/cholesky | solution.py:39
  302.1 12.1 %cholesky.305 = f32[128,128]{1,0:T(8,128)S(1)} custom-call(f32[128,128]{1,0:T(8,128)S(1)} %cholesky.430), custom_call_target="Cholesky" | custom-call | tf_op jit(solution)/shard_map/jit(cholesky)/cholesky | solution.py:39
  314.2 9.8 %custom-call.34 = f32[1,128,128]{1,2,0:T(8,128)S(1)} custom-call(f32[1,128,128]{2,1,0:T(8,128)S(1)} %get-tuple-element.69), custom_call_target="InvertDiagBlocksLowerTriangular" | custom-call | tf_op jit(solution)/shard_map/jit(cholesky)/cholesky | solution.py:39
  325.6 11.7 %cholesky.326 = f32[128,128]{1,0:T(8,128)S(1)} custom-call(f32[128,128]{1,0:T(8,128)S(1)} %cholesky.435), custom_call_target="Cholesky" | custom-call | tf_op jit(solution)/shard_map/jit(cholesky)/cholesky | solution.py:39
  338.0 9.8 %custom-call.35 = f32[1,128,128]{1,2,0:T(8,128)S(1)} custom-call(f32[1,128,128]{2,1,0:T(8,128)S(1)} %get-tuple-element.66), custom_call_target="InvertDiagBlocksLowerTriangular" | custom-call | tf_op jit(solution)/shard_map/jit(cholesky)/cholesky | solution.py:39
  349.2 11.9 %cholesky.343 = f32[128,128]{1,0:T(8,128)S(1)} custom-call(f32[128,128]{1,0:T(8,128)S(1)} %convolution_subtract_fusion.17), custom_call_target="Cholesky" | custom-call | tf_op jit(solution)/shard_map/jit(cholesky)/cholesky | solution.py:39
  365.1 7.8 %while.4 = (s32[]{:T(128)}, f32[512,512]{1,0:T(8,128)S(1)}, s32[4,2]{0,1:T(2,128)S(1)}, f32[4,128,128]{2,1,0:T(8,128)S(1)}, s32[]{:T(128)}) while((s32[]{:T(128)}, f32[512,512]{1,0:T(8,128)S(1)}, s32[4,2]{0,1:T(2,128)S(1)}, f32[4,128,128]{2,1,0:T(8,128)S(1)}, s32[]{:T(128)}) %tuple.56), condition=%wide.while_cond, body=%wide.while_body.sunk | while | flops 2 | bytes 131181 | solution.py:40
  372.9 39.3 %custom-call.36 = f32[4,128,128]{1,2,0:T(8,128)S(1)} custom-call(f32[4,128,128]{2,1,0:T(8,128)S(1)} %get-tuple-element.21), custom_call_target="InvertDiagBlocksLowerTriangular" | custom-call | tf_op jit(solution)/shard_map/jit(_cho_solve)/triangular_solve | solution.py:40
  418.4 12.8 %fusion.11 = f32[3072,512]{0,1:T(8,128)S(1)} fusion(f32[3072,512]{1,0:T(8,128)} %bitcast.145, f32[128,512]{1,0:T(8,128)S(1)} %fusion.103, f32[128,512]{1,0:T(8,128)S(1)} %fusion.101, f32[128,512]{1,0:T(8,128)S(1)} %fusion.99, f32[128,512]{1,0:T(8,128)S(1)} %fusion.98), kind=kOutput, calls=%fused_computation.53 | convolution fusion | flops 9664462848 | bytes 13631488 | tf_op jit(solution)/shard_map/dot_general | solution.py:41
  431.3 2.5 slice_select_fusion.2
  434.9 1.9 collective-permute-start
  436.8 3.6 collective-permute-start.1
  440.5 33.3 %collective-permute-done = f32[3072,256]{0,1:T(8,128)} collective-permute-done((f32[3072,256]{0,1:T(8,128)}, f32[3072,256]{0,1:T(8,128)}, u32[]{:S(2)}, u32[]{:S(2)}) %collective-permute-start) | collective-permute-done | bytes 3145760 | tf_op jit(solution)/shard_map/ppermute | solution.py:17
  473.8 1.4 collective-permute-done.1
  475.2 4.5 slice_select_fusion.1
  479.8 1.6 copy-done.2
  481.5 11.7 %fusion.3 = f32[512,512]{0,1:T(8,128)} fusion(f32[3072,256]{0,1:T(8,128)S(1)} %get-tuple-element.46, f32[3072,256]{0,1:T(8,128)S(1)} %get-tuple-element.45), kind=kOutput, calls=%fused_computation.13 | convolution fusion | flops 9665249280 | bytes 7340032 | tf_op jit(solution)/shard_map/dot_general | solution.py:21
  493.5 52.9 %all-reduce.6.cloned.1.call-done = f32[512,512]{0,1:T(8,128)} async-done(((f32[512,512]{0,1:T(8,128)}), f32[512,512]{0,1:T(8,128)}) %all-reduce.6.cloned.1.call-update) | async-done | bytes 1048592 | tf_op jit(solution)/shard_map/psum | solution.py:28
  546.5 8.9 %gather_fusion.2 = f32[512]{0:T(512)S(1)} fusion(f32[512,512]{0,1:T(8,128)} %all-reduce.6.cloned.1.call-done, s32[512]{0:T(512)S(1)} %bitcast.141), kind=kCustom, calls=%fused_computation.2 | custom fusion | bytes 8192 | tf_op jit(solution)/shard_map/jit(diagonal)/cond/branch_0_fun/gather | solution.py:29
  555.4 4.0 convolution_multiply_fusion
  559.5 1.8 convert_subtract_fusion
  561.2 2.6 copy.46
  563.8 1.8 fusion.26
  566.6 11.7 %cholesky.358 = f32[128,128]{1,0:T(8,128)S(1)} custom-call(f32[128,128]{1,0:T(8,128)S(1)} %cholesky.439), custom_call_target="Cholesky" | custom-call | tf_op jit(solution)/shard_map/jit(cholesky)/cholesky | solution.py:39
  579.4 9.8 %custom-call.37 = f32[1,128,128]{1,2,0:T(8,128)S(1)} custom-call(f32[1,128,128]{2,1,0:T(8,128)S(1)} %get-tuple-element.62), custom_call_target="InvertDiagBlocksLowerTriangular" | custom-call | tf_op jit(solution)/shard_map/jit(cholesky)/cholesky | solution.py:39
  589.2 1.9 constant_dynamic-update-slice_fusion.3
  592.4 11.9 %cholesky.377 = f32[128,128]{1,0:T(8,128)S(1)} custom-call(f32[128,128]{1,0:T(8,128)S(1)} %cholesky.443), custom_call_target="Cholesky" | custom-call | tf_op jit(solution)/shard_map/jit(cholesky)/cholesky | solution.py:39
  606.3 9.8 %custom-call.38 = f32[1,128,128]{1,2,0:T(8,128)S(1)} custom-call(f32[1,128,128]{2,1,0:T(8,128)S(1)} %get-tuple-element.59), custom_call_target="InvertDiagBlocksLowerTriangular" | custom-call | tf_op jit(solution)/shard_map/jit(cholesky)/cholesky | solution.py:39
  617.0 1.4 convolution_subtract_fusion.14
  618.5 11.7 %cholesky.398 = f32[128,128]{1,0:T(8,128)S(1)} custom-call(f32[128,128]{1,0:T(8,128)S(1)} %cholesky.448), custom_call_target="Cholesky" | custom-call | tf_op jit(solution)/shard_map/jit(cholesky)/cholesky | solution.py:39
  631.5 9.8 %custom-call.39 = f32[1,128,128]{1,2,0:T(8,128)S(1)} custom-call(f32[1,128,128]{2,1,0:T(8,128)S(1)} %get-tuple-element.56), custom_call_target="InvertDiagBlocksLowerTriangular" | custom-call | tf_op jit(solution)/shard_map/jit(cholesky)/cholesky | solution.py:39
  642.2 1.4 convolution_subtract_fusion.16
  643.6 11.9 %cholesky.415 = f32[128,128]{1,0:T(8,128)S(1)} custom-call(f32[128,128]{1,0:T(8,128)S(1)} %convolution_subtract_fusion.16), custom_call_target="Cholesky" | custom-call | tf_op jit(solution)/shard_map/jit(cholesky)/cholesky | solution.py:39
  659.4 2.3 select_select_fusion
  661.7 11.4 %while.5 = (s32[]{:T(128)}, f32[512,512]{1,0:T(8,128)}, s32[4,2]{0,1:T(2,128)S(1)}, f32[4,128,128]{2,1,0:T(8,128)S(1)}, s32[]{:T(128)}) while((s32[]{:T(128)}, f32[512,512]{1,0:T(8,128)}, s32[4,2]{0,1:T(2,128)S(1)}, f32[4,128,128]{2,1,0:T(8,128)S(1)}, s32[]{:T(128)}) %tuple.66), condition=%wide.while_cond.clone, body=%wide.while_body.clone.sunk | while | flops 2 | bytes 131181 | solution.py:40
  662.4 2.2 bitcast_dynamic-update-slice_fusion.5
  665.2 2.2 bitcast_dynamic-update-slice_fusion.5
  668.1 2.2 bitcast_dynamic-update-slice_fusion.5
  671.0 2.2 bitcast_dynamic-update-slice_fusion.5
  673.8 40.1 %custom-call.40 = f32[4,128,128]{1,2,0:T(8,128)S(1)} custom-call(f32[4,128,128]{2,1,0:T(8,128)} %copy-done.10), custom_call_target="InvertDiagBlocksLowerTriangular" | custom-call | tf_op jit(solution)/shard_map/jit(_cho_solve)/triangular_solve | solution.py:40
  714.0 1.5 fusion.60
  715.5 1.4 convolution_subtract_fusion.3
  717.3 1.4 convolution_subtract_fusion.2
  719.2 1.7 convolution_subtract_fusion.9
  723.3 1.4 convolution_subtract_fusion
  725.1 1.6 convolution_subtract_fusion.8
  727.0 22.3 %fusion.2 = f32[3072,512]{1,0:T(8,128)} fusion(f32[3072,256]{0,1:T(8,128)S(1)} %copy-done.3, f32[3072,256]{0,1:T(8,128)S(1)} %get-tuple-element.45, f32[128,512]{1,0:T(8,128)S(1)} %fusion.110, f32[128,512]{1,0:T(8,128)S(1)} %fusion.108, f32[128,512]{1,0:T(8,128)S(1)} %fusion.106, f32[128,512]{1,0:T(8,128)S(1)} %fusion.105), kind=kOutput, calls=%fused_computation.12 | convolution fusion | flops 9666035712 | bytes 13631488 | tf_op jit(solution)/shard_map/dot_general | solution.py:41
  749.4 6.8 gather_fusion.3
  756.2 1.5 broadcast_select_fusion.1
  (127 shorter events, 45.3 us)
Async XLA Ops:
  6.5 255.5 %all-reduce.4.cloned.1.call-start = ((), (), s32[]{:S(2)}) async-start(), calls=%async_computation.1 | async-start | bytes 2097152 | tf_op jit(solution)/shard_map/psum | solution.py:28
  16.4 6.5 copy-start.11
  193.6 2.7 copy-start.1
  207.7 338.8 %all-reduce.6.cloned.1.call-start = ((), (), s32[]{:S(2)}) async-start(), calls=%async_computation.2 | async-start | bytes 2097152 | tf_op jit(solution)/shard_map/psum | solution.py:28
  262.0 12.9 %copy-start.5 = (f32[512,512]{0,1:T(8,128)S(1)}, f32[512,512]{0,1:T(8,128)}, u32[]{:S(2)}) copy-start(f32[512,512]{0,1:T(8,128)} %all-reduce.4.cloned.1.call-done) | copy-start | bytes 3145732
  276.6 135.6 %copy-start.7 = (f32[512,512]{1,0:T(8,128)S(1)}, f32[512,512]{1,0:T(8,128)}, u32[]{:S(2)}) copy-start(f32[512,512]{1,0:T(8,128)} %get-tuple-element.52) | copy-start | bytes 3145732
  276.8 1.0 copy-start.9
  431.3 3.6 copy-start
  434.9 38.9 %collective-permute-start = (f32[3072,256]{0,1:T(8,128)}, f32[3072,256]{0,1:T(8,128)}, u32[]{:S(2)}, u32[]{:S(2)}) collective-permute-start(f32[3072,256]{0,1:T(8,128)} %get-tuple-element.47), channel_id=1, source_target_pairs={{0,1},{1,2},{2,3},{3,4},{4,5},{5,6},{6,7},{8,9},{9,10},{10,11},{11... | collective-permute-start | bytes 9437192 | tf_op jit(solution)/shard_map/ppermute | solution.py:17
  436.8 38.4 %collective-permute-start.1 = (f32[3072,256]{0,1:T(8,128)S(1)}, f32[3072,256]{0,1:T(8,128)}, u32[]{:S(2)}, u32[]{:S(2)}) collective-permute-start(f32[3072,256]{0,1:T(8,128)S(1)} %get-tuple-element.48), channel_id=1, source_target_pairs={{1,0},{2,1},{3,2},{4,3},{5,4},{6,5},{7,6},{9,8},{10,9},{11,10},{12... | collective-permute-start | bytes 9437192 | tf_op jit(solution)/shard_map/ppermute | solution.py:17
  479.8 1.7 copy-start.2
  479.8 13.4 %copy-start.12 = (s32[1,8]{1,0:T(1,128)S(1)}, s32[1,8]{1,0:T(1,128)}, u32[]{:S(2)}) copy-start(s32[1,8]{1,0:T(1,128)} %param.8) | copy-start | bytes 100
  555.4 4.0 copy-start.4
  559.4 1.8 copy-start.6
  565.6 1.0 copy-start.8
  673.1 0.7 copy-start.10
  714.0 13.1 %copy-start.3 = (f32[3072,256]{0,1:T(8,128)S(1)}, f32[3072,256]{0,1:T(8,128)}, u32[]{:S(2)}) copy-start(f32[3072,256]{0,1:T(8,128)} %copy-done.2) | copy-start | bytes 9437188
Sparse Core Ops, SparseCore 0:
  207.8 54.1 all-reduce.3
  493.3 53.1 all-reduce.5
where the time goes:
time: 772 us; the launch traced here: 765 us
  other arithmetic  269 us (35%)
  waiting for transfers between devices  142 us (18%)
  blocking collectives  141 us (18%)
  matrix products  98.7 us (13%)
  local copies, waits for them, and re-layouts  88.6 us (11%)
  between operations  19.6 us (3%)
    another operation x29, other arithmetic, rotate(): factor = jnp.linalg.cholesky(sym_part)  160 us
    all_to_all x1, blocking collectives, local(): lax.all_to_all(seated, 'pairs', split_axis=1, concat_axis=0, tiled=True)  141 us
    psum x2, waiting for transfers between devices, rotate(): gram_full = lax.psum(partial_gram, 'rows')  107 us
    another operation x5, other arithmetic, rotate(): transposed = jax.scipy.linalg.cho_solve((factor, True), numerator.T)  81.9 us
    dot_general x2, matrix products, rotate(): return jnp.dot(panels, transposed.T, precision=lax.Precision.HIGHEST)  35.2 us
    ppermute x2, waiting for transfers between devices, passed_along(): return lax.ppermute(array, axis, pairs)  34.8 us
    dot_general x2, matrix products, rotate(): lax.dot_general(panels, panels, (((0,), (0,)), ((), ())), precision=lax.P...  23.1 us
    gather x3, local copies, waits for them, and re-layouts, local(): jnp.take(scaled.reshape(capacity, columns // BLOCK, BLOCK), seating, axis=1)  19.5 us
  transfers between devices with their start and end apart: 4, of which 4 were waited for; matrix products, arithmetic and copies ran while one was open for 0% of the time, Pallas kernels for 0%

commit v1 on v0

v1 whole, which is shorter than its diff:
```python
import functools

import jax
import jax.numpy as jnp
from jax import lax
from jax.experimental import pallas as pl
from jax.experimental.pallas import tpu as pltpu
from jax.sharding import PartitionSpec as P

ROWS_DEV = 1024
BLOCK = 256
ROUNDS = 2
WIDTH = 2 * BLOCK
TILE = 128
ALIGN = 8
MARGIN = 16
CHUNKS = 4
NEWTON_STEPS = 18
SERIES_BOUND = 1e-6
VMEM_LIMIT = 48 * 1024 * 1024

epsilon = 1e-06

MESH = pl.DeviceIdType.MESH
TILE_PAIRS = [(i, j) for i in range(WIDTH // TILE) for j in range(i, WIDTH // TILE)]
PACKED = len(TILE_PAIRS) * TILE


def halves(x):
    high = x.astype(jnp.bfloat16)
    low = (x - high.astype(jnp.float32)).astype(jnp.bfloat16)
    return high, low


def dot_halves(a, b):
    mul = functools.partial(jnp.dot, preferred_element_type=jnp.float32)
    return mul(a[0], b[0]) + (mul(a[0], b[1]) + mul(a[1], b[0]))


def dot_three(a, b):
    return dot_halves(halves(a), halves(b))


def add_gram(main, cross, block):
    high, low = halves(block)
    mul = functools.partial(
        lax.dot_general,
        dimension_numbers=(((0,), (0,)), ((), ())),
        preferred_element_type=jnp.float32,
    )
    main[...] += mul(high, high)
    cross[...] += mul(high, low)


def pack_gram(main, cross, packed):
    for t, (i, j) in enumerate(TILE_PAIRS):
        rows, cols = pl.ds(i * TILE, TILE), pl.ds(j * TILE, TILE)
        packed[pl.ds(t * TILE, TILE), :] = (
            main[rows, cols] + cross[rows, cols] + cross[cols, rows].T
        )


def remote(src, dst, send_sem, recv_sem, axis, index):
    return pltpu.make_async_remote_copy(
        src_ref=src,
        dst_ref=dst,
        send_sem=send_sem,
        recv_sem=recv_sem,
        device_id={axis: index},
        device_id_type=MESH,
    )


def signal_peers(barrier, axis, count):
    mine = lax.axis_index(axis)
    for d in range(1, count):
        pl.semaphore_signal(
            barrier,
            inc=1,
            device_id={axis: lax.rem(mine + d, count)},
            device_id_type=MESH,
        )


def sum_over_rows(count, packed, parts, total, scatter_send, scatter_recv, gather_send, gather_recv, between):
    mine = lax.axis_index("rows")
    share = PACKED // count

    def part(index):
        return pl.ds(pl.multiple_of(index * share, 8), share)

    scatter = []
    for d in range(1, count):
        peer = lax.rem(mine + d, count)
        copy = remote(packed.at[part(peer)], parts.at[d - 1], scatter_send.at[d - 1], scatter_recv.at[d - 1], "rows", peer)
        copy.start()
        scatter.append(copy)
    between()
    summed = packed[part(mine), :]
    for d in range(1, count):
        scatter[d - 1].wait_recv()
        summed = summed + parts[d - 1]
    total[part(mine), :] = summed
    gather = []
    for d in range(1, count):
        peer = lax.rem(mine + d, count)
        copy = remote(total.at[part(mine)], total.at[part(mine)], gather_send.at[d - 1], gather_recv.at[d - 1], "rows", peer)
        copy.start()
        gather.append(copy)
    for d in range(1, count):
        source = lax.rem(mine + count - d, count)
        remote(total.at[part(source)], total.at[part(source)], gather_send.at[d - 1], gather_recv.at[d - 1], "rows", source).wait_recv()
    for copy in scatter + gather:
        copy.wait_send()


def seat_kernel(pairs, seating_ref, counts_ref, unit_ref, scale_ref, out_ref):
    mine = lax.axis_index("pairs")
    start = jnp.int32(0)
    for k in range(pairs):
        start = start + jnp.where(k < mine, counts_ref[0, k], 0)
    block = unit_ref[0, 0]
    live = lax.broadcasted_iota(jnp.int32, block.shape, 0) < counts_ref[0, mine]
    scaled = jnp.where(live, block * scale_ref[...], 0.0)
    margin = jnp.zeros((out_ref.shape[1] - block.shape[0], BLOCK), jnp.float32)
    out_ref[0] = pltpu.roll(jnp.concatenate([scaled, margin], axis=0), start & (ALIGN - 1), 0)


def seat(pairs, unit_rows, channel_scale, seating, unit_counts):
    capacity, columns = unit_rows.shape[2:]
    room = capacity + MARGIN
    return pl.pallas_call(
        functools.partial(seat_kernel, pairs),
        out_shape=jax.ShapeDtypeStruct((pairs, room, WIDTH), jnp.float32),
        grid_spec=pltpu.PrefetchScalarGridSpec(
            num_scalar_prefetch=2,
            grid=(2 * pairs,),
            in_specs=[
                pl.BlockSpec((1, 1, capacity, BLOCK), lambda i, seating, counts: (0, 0, 0, seating[i])),
                pl.BlockSpec((1, BLOCK), lambda i, seating, counts: (0, seating[i])),
            ],
            out_specs=pl.BlockSpec((1, room, BLOCK), lambda i, seating, counts: (i // 2, 0, i % 2)),
        ),
        compiler_params=pltpu.CompilerParams(vmem_limit_bytes=VMEM_LIMIT),
        name="seat",
    )(seating, unit_counts, unit_rows, channel_scale)


def collect_kernel(
    pairs, rows, room,
    seated, units_ref, gram_ref,
    landed, main, cross, packed, parts, total,
    send_sem, recv_sem, keep_sem, out_sem, scatter_send, scatter_recv, gather_send, gather_recv,
):
    mine = lax.axis_index("pairs")
    barrier = pltpu.get_barrier_semaphore()
    signal_peers(barrier, "pairs", pairs)
    signal_peers(barrier, "rows", rows)
    keep = pltpu.make_async_copy(seated.at[mine], landed.at[mine], keep_sem)
    keep.start()
    main[...] = jnp.zeros_like(main)
    cross[...] = jnp.zeros_like(cross)
    pl.semaphore_wait(barrier, pairs + rows - 2)

    def copy_to(d):
        peer = lax.rem(mine + d, pairs)
        return remote(seated.at[peer], landed.at[mine], send_sem.at[d - 1], recv_sem.at[d - 1], "pairs", peer)

    def write_out(source, d):
        return pltpu.make_async_copy(landed.at[source], units_ref.at[source], out_sem.at[d])

    def send(d, carry):
        copy_to(d).start()
        return carry

    lax.fori_loop(1, pairs, send, 0)
    keep.wait()
    write_out(mine, 0).start()
    add_gram(main, cross, landed[mine])

    def receive(d, carry):
        source = lax.rem(mine + pairs - d, pairs)
        remote(seated.at[source], landed.at[source], send_sem.at[d - 1], recv_sem.at[d - 1], "pairs", source).wait_recv()
        write_out(source, d).start()
        add_gram(main, cross, landed[source])
        return carry

    lax.fori_loop(1, pairs, receive, 0)
    pack_gram(main, cross, packed)
    sum_over_rows(rows, packed, parts, total, scatter_send, scatter_recv, gather_send, gather_recv, lambda: None)
    gram_ref[...] = total[...]
    write_out(mine, 0).wait()

    def finish(d, carry):
        copy_to(d).wait_send()
        write_out(lax.rem(mine + pairs - d, pairs), d).wait()
        return carry

    lax.fori_loop(1, pairs, finish, 0)


def gram_scratch(rows):
    return [
        pltpu.VMEM((WIDTH, WIDTH), jnp.float32),
        pltpu.VMEM((WIDTH, WIDTH), jnp.float32),
        pltpu.VMEM((PACKED, TILE), jnp.float32),
        pltpu.VMEM((rows - 1, PACKED // rows, TILE), jnp.float32),
        pltpu.VMEM((PACKED, TILE), jnp.float32),
    ]


def row_sems(rows):
    return [pltpu.SemaphoreType.DMA((rows - 1,))] * 4


ANY_SPEC = pl.BlockSpec(memory_space=pl.ANY)
VMEM_SPEC = pl.BlockSpec(memory_space=pltpu.VMEM)
SMEM_SPEC = pl.BlockSpec(memory_space=pltpu.SMEM)
PANEL_AND_GRAM = (
    jax.ShapeDtypeStruct((ROWS_DEV, WIDTH), jnp.float32),
    jax.ShapeDtypeStruct((PACKED, TILE), jnp.float32),
)


def collect(pairs, rows, seated):
    return pl.pallas_call(
        functools.partial(collect_kernel, pairs, rows, seated.shape[1]),
        out_shape=(
            jax.ShapeDtypeStruct(seated.shape, jnp.float32),
            jax.ShapeDtypeStruct((PACKED, TILE), jnp.float32),
        ),
        in_specs=[ANY_SPEC],
        out_specs=(ANY_SPEC, VMEM_SPEC),
        scratch_shapes=[
            pltpu.VMEM(seated.shape, jnp.float32),
            *gram_scratch(rows),
            pltpu.SemaphoreType.DMA((pairs - 1,)),
            pltpu.SemaphoreType.DMA((pairs - 1,)),
            pltpu.SemaphoreType.DMA,
            pltpu.SemaphoreType.DMA((pairs,)),
            *row_sems(rows),
        ],
        compiler_params=pltpu.CompilerParams(
            collective_id=0, has_side_effects=True, vmem_limit_bytes=VMEM_LIMIT
        ),
        name="collect",
    )(seated)


def exchange_kernel(
    pairs, rows,
    old_ref, panel_ref, gram_ref,
    landed, main, cross, packed, parts, total,
    up_send, up_recv, down_send, down_recv, scatter_send, scatter_recv, gather_send, gather_recv,
):
    mine = lax.axis_index("pairs")
    last = pairs - 1
    barrier = pltpu.get_barrier_semaphore()
    signal_peers(barrier, "rows", rows)

    def greet(index):
        pl.semaphore_signal(barrier, inc=1, device_id={"pairs": index}, device_id_type=MESH)

    @pl.when(mine < last)
    def _():
        greet(mine + 1)

    @pl.when(mine > 0)
    def _():
        greet(mine - 1)

    main[...] = jnp.zeros_like(main)
    cross[...] = jnp.zeros_like(cross)
    greeted = jnp.where(mine < last, 1, 0) + jnp.where(mine > 0, 1, 0)
    pl.semaphore_wait(barrier, rows - 1 + greeted)

    size = ROWS_DEV // CHUNKS
    upper, lower = pl.ds(0, BLOCK), pl.ds(BLOCK, BLOCK)

    def up(c, source):
        here = pl.ds(c * size, size)
        return remote(old_ref.at[here, source], landed.at[here, upper], up_send.at[c], up_recv.at[c], "pairs", mine + 1)

    def down(c):
        here = pl.ds(c * size, size)
        return remote(old_ref.at[here, lower], landed.at[here, lower], down_send.at[c], down_recv.at[c], "pairs", mine - 1)

    for c in range(CHUNKS):
        @pl.when(mine == 0)
        def _():
            up(c, lower).start()

        @pl.when((mine > 0) & (mine < last))
        def _():
            up(c, upper).start()

        @pl.when(mine > 0)
        def _():
            down(c).start()

    @pl.when(mine == 0)
    def _():
        landed[:, upper] = old_ref[:, upper]

    @pl.when(mine == last)
    def _():
        landed[:, lower] = old_ref[:, upper]

    for c in range(CHUNKS):
        @pl.when(mine > 0)
        def _():
            up(c, upper).wait_recv()

        @pl.when(mine < last)
        def _():
            down(c).wait_recv()

        add_gram(main, cross, landed[pl.ds(c * size, size), :])
    pack_gram(main, cross, packed)

    def hand_over():
        panel_ref[...] = landed[...]

    sum_over_rows(rows, packed, parts, total, scatter_send, scatter_recv, gather_send, gather_recv, hand_over)
    gram_ref[...] = total[...]
    for c in range(CHUNKS):
        @pl.when(mine < last)
        def _():
            up(c, upper).wait_send()

        @pl.when(mine > 0)
        def _():
            down(c).wait_send()


def exchange(pairs, rows, panel):
    return pl.pallas_call(
        functools.partial(exchange_kernel, pairs, rows),
        out_shape=PANEL_AND_GRAM,
        in_specs=[VMEM_SPEC],
        out_specs=(VMEM_SPEC, VMEM_SPEC),
        scratch_shapes=[
            pltpu.VMEM((ROWS_DEV, WIDTH), jnp.float32),
            *gram_scratch(rows),
            *[pltpu.SemaphoreType.DMA((CHUNKS,))] * 4,
            *row_sems(rows),
        ],
        compiler_params=pltpu.CompilerParams(
            collective_id=1, has_side_effects=True, vmem_limit_bytes=VMEM_LIMIT
        ),
        name="exchange",
    )(panel)


def turn_units_kernel(counts_ref, packed, units_ref, out, units, panel, load_sem, *scratch):
    pairs, room = units.shape[:2]
    load = pltpu.make_async_copy(units_ref, units, load_sem)
    load.start()

    def compact():
        load.wait()
        start = jnp.int32(0)
        head = lax.broadcasted_iota(jnp.int32, (ALIGN, WIDTH), 0)
        for k in range(pairs):
            first = pl.multiple_of(start & -ALIGN, ALIGN)
            top = pl.ds(first, ALIGN)
            panel[top, :] = jnp.where(head < (start & (ALIGN - 1)), panel[top, :], units[k, pl.ds(0, ALIGN), :])
            panel[pl.ds(pl.multiple_of(first + ALIGN, ALIGN), room - ALIGN), :] = units[k, pl.ds(ALIGN, room - ALIGN), :]
            start = start + counts_ref[0, k]

    turn_panel(packed, panel, out, compact, *scratch)


def turn_kernel(packed, panel, out, *scratch):
    turn_panel(packed, panel, out, lambda: None, *scratch)


def turn_panel(packed, panel, out, prepare, gram, tangent, square, change):
    on_diag = lax.broadcasted_iota(jnp.int32, (TILE, TILE), 0) == lax.broadcasted_iota(jnp.int32, (TILE, TILE), 1)
    across, along = [], []
    for t, (i, j) in enumerate(TILE_PAIRS):
        tile = packed[pl.ds(t * TILE, TILE), :]
        gram[pl.ds(i * TILE, TILE), pl.ds(j * TILE, TILE)] = tile
        if i == j:
            kept = jnp.where(on_diag, tile, 0.0)
            across.append(jnp.sum(kept, axis=0, keepdims=True))
            along.append(jnp.sum(kept, axis=1, keepdims=True))
        else:
            gram[pl.ds(j * TILE, TILE), pl.ds(i * TILE, TILE)] = tile.T
    diag_row = jnp.concatenate(across, axis=1)
    diag_col = jnp.concatenate(along, axis=0)
    tangent[...] = 0.5 * (
        gram[...] * (diag_row - diag_col) / (2.0 * (diag_col**2 + diag_row**2) + epsilon)
    )
    t_halves = halves(tangent[...])
    square[...] = dot_halves(t_halves, t_halves)
    m_halves = halves(square[...])
    fourth = dot_halves(m_halves, m_halves)
    rest = jnp.sum(fourth * fourth)
    short = rest <= SERIES_BOUND

    @pl.when(short)
    def _():
        first = tangent[...] + square[...]
        second = first + dot_halves(halves(first), m_halves)
        change[...] = 2.0 * (second + dot_three(second, fourth))

    @pl.when(jnp.logical_not(short))
    def _():
        exact = functools.partial(
            jnp.dot, precision=lax.Precision.HIGHEST, preferred_element_type=jnp.float32
        )
        eye = (
            lax.broadcasted_iota(jnp.int32, (WIDTH, WIDTH), 0)
            == lax.broadcasted_iota(jnp.int32, (WIDTH, WIDTH), 1)
        )
        square[...] = exact(tangent[...], tangent[...])
        bound = jnp.sqrt(jnp.sqrt(jnp.full((1, 1), rest, jnp.float32))) * 1.01
        change[...] = jnp.where(eye, 2.0 / (2.0 + bound), 0.0)

        def newton(step, carry):
            inverse = change[...]
            residual = jnp.where(eye, 1.0, 0.0) - inverse + exact(square[...], inverse)
            change[...] = inverse + exact(inverse, residual)
            return carry

        lax.fori_loop(0, NEWTON_STEPS, newton, 0)
        change[...] = 2.0 * exact(tangent[...] + square[...], change[...])

    prepare()
    d_halves = halves(change[...])
    size = ROWS_DEV // CHUNKS

    def apply(c, carry):
        here = pl.ds(pl.multiple_of(c * size, size), size)
        block = panel[here, :]
        out[here, :] = block + dot_halves(halves(block), d_halves)
        return carry

    lax.fori_loop(0, CHUNKS, apply, 0)


def turn_units(unit_counts, packed, units):
    pairs, room = units.shape[:2]
    return pl.pallas_call(
        turn_units_kernel,
        out_shape=PANEL_AND_GRAM[0],
        in_specs=[SMEM_SPEC, VMEM_SPEC, ANY_SPEC],
        out_specs=VMEM_SPEC,
        scratch_shapes=[
            pltpu.VMEM(units.shape, jnp.float32),
            pltpu.VMEM((ROWS_DEV + room, WIDTH), jnp.float32),
            pltpu.SemaphoreType.DMA,
            *[pltpu.VMEM((WIDTH, WIDTH), jnp.float32)] * 4,
        ],
        compiler_params=pltpu.CompilerParams(vmem_limit_bytes=VMEM_LIMIT),
        name="turn_units",
    )(unit_counts, packed, units)


def turn(packed, panel):
    return pl.pallas_call(
        turn_kernel,
        out_shape=PANEL_AND_GRAM[0],
        in_specs=[VMEM_SPEC, VMEM_SPEC],
        out_specs=VMEM_SPEC,
        scratch_shapes=[pltpu.VMEM((WIDTH, WIDTH), jnp.float32)] * 4,
        compiler_params=pltpu.CompilerParams(vmem_limit_bytes=VMEM_LIMIT),
        name="turn",
    )(packed, panel)


def local(pairs, rows, unit_rows, unit_counts, seating, channel_scale):
    seated = seat(pairs, unit_rows, channel_scale[None, :], seating, unit_counts)
    units, gram = collect(pairs, rows, seated)
    panel = turn_units(unit_counts, gram, units)
    for round_index in range(1, ROUNDS):
        panel, gram = exchange(pairs, rows, panel)
        panel = turn(gram, panel)
    return panel


def solution(mesh):
    return jax.shard_map(
        functools.partial(local, mesh.shape["pairs"], mesh.shape["rows"]),
        mesh=mesh,
        in_specs=(P("rows", "pairs", None, None), P("rows", None), P(), P()),
        out_specs=P("rows", "pairs"),
        check_vma=False,
    )
```

time: 772 us -> 362 us (0.47)
  Pallas kernels: 0 us -> 359 us
  other arithmetic: 269 us -> 0 us
  waiting for transfers between devices: 142 us -> 0 us
  blocking collectives: 141 us -> 0 us
  matrix products: 98.7 us -> 0 us
  local copies, waits for them, and re-layouts: 88.6 us -> 2.03 us
  between operations: 19.6 us -> 0.04 us
    pallas_call x0 -> x5, Pallas kernels: none -> 359 us  [the longest x1 144 us: collect(): pl.pallas_call(functools.partial(collect_kernel, pairs, rows, seated.shap...]
    another operation x35 -> x0, other arithmetic: 242 us -> none  [the longest x29 160 us: rotate(): factor = jnp.linalg.cholesky(sym_part)]
    all_to_all x1 -> x0, blocking collectives: 141 us -> none  [local(): lax.all_to_all(seated, 'pairs', split_axis=1, concat_axis=0, tiled=True)]
    psum x2 -> x0, waiting for transfers between devices: 107 us -> none  [rotate(): gram_full = lax.psum(partial_gram, 'rows')]
    dot_general x6 -> x0, matrix products: 66.4 us -> none  [the longest x2 35.2 us: rotate(): return jnp.dot(panels, transposed.T, precision=lax.Precision.HIGHEST)]
    gather x6 -> x0, local copies, waits for them, and re-layouts: 44 us -> none  [the longest x3 19.5 us: local(): jnp.take(scaled.reshape(capacity, columns // BLOCK, BLOCK), seating, axis=1)]
    ppermute x2 -> x0, waiting for transfers between devices: 34.8 us -> none  [passed_along(): return lax.ppermute(array, axis, pairs)]
    another operation x40 -> x0, matrix products: 32.3 us -> none  [the longest x28 19.1 us: rotate(): transposed = jax.scipy.linalg.cho_solve((factor, True), numerator.T)]
  transfers between devices with their start and end apart: 4 -> 0, of which waited for: 4 -> 0; matrix products, arithmetic and copies ran while one was open for 0% -> 0% of each run, Pallas kernels for 0% -> 0%
where the time goes in v1:
time: 362 us; the launch traced here: 361 us
  Pallas kernels  359 us (99%)
    pallas_call x1, Pallas kernels, collect(): pl.pallas_call(functools.partial(collect_kernel, pairs, rows, seated.shap...  144 us
    pallas_call x1, Pallas kernels, turn(): pl.pallas_call(turn_kernel, out_shape=PANEL_AND_GRAM[0], in_specs=[VMEM_S...  77 us
    pallas_call x1, Pallas kernels, turn_units(): pl.pallas_call(turn_units_kernel, out_shape=PANEL_AND_GRAM[0], in_specs=[...  76.8 us
    pallas_call x1, Pallas kernels, exchange(): pl.pallas_call(functools.partial(exchange_kernel, pairs, rows), out_shape...  48.3 us
    pallas_call x1, Pallas kernels, seat(): pl.pallas_call(functools.partial(seat_kernel, pairs), out_shape=jax.Shape...  13.6 us

profile of v1, /device:TPU:16, one launch (start us, length us, event | category | flops | bytes accessed | tf_op | source)
XLA Modules:
  0.0 361.3 jit_solution(14772809910580794856)
XLA Ops:
  0.0 0.0 copy-start
  0.0 0.7 copy-done
  0.7 0.0 copy-start.1
  0.7 0.7 copy-done.1
  1.4 0.0 copy-start.3
  1.4 0.7 copy-done.3
  2.0 13.6 %seat.1.seated = f32[8,400,512]{2,1,0:T(8,128)} custom-call(s32[16]{0:T(128)S(1)} %copy-done.3, s32[1,8]{1,0:T(1,128)S(1)} %copy-done.1, f32[1,1,384,4096]{3,2,1,0:T(8,128)} %unit_ref.1, f32[1,4096]{1,0:T(1,128)S(1)} %bitcast.1), custom_call_target="tpu_custom_call" | custom-call | tf_op jit(solution)/shard_map/seat/pallas_call | solution.py:132
  15.6 0.0 copy-start.2
  15.6 143.5 %collect.1 = (f32[8,400,512]{2,1,0:T(8,128)}, f32[1280,128]{1,0:T(8,128)S(1)}) custom-call(f32[8,400,512]{2,1,0:T(8,128)} %seat.1.seated), custom_call_target="tpu_custom_call" | custom-call | tf_op jit(solution)/shard_map/collect/pallas_call | solution.py:226
  159.2 0.0 copy-done.2
  159.2 76.8 %turn_units.1.old_ref = f32[1024,512]{1,0:T(8,128)S(1)} custom-call(s32[1,8]{1,0:T(1,128)S(1)} %copy-done.2, f32[1280,128]{1,0:T(8,128)S(1)} %get-tuple-element.9.packed, f32[8,400,512]{2,1,0:T(8,128)} %get-tuple-element.10.units_ref), custom_call_target="tpu_custom_call" | custom-call | tf_op jit(solution)/shard_map/turn_units/pallas_call | solution.py:445
  236.0 48.3 %exchange.1 = (f32[1024,512]{1,0:T(8,128)S(1)}, f32[1280,128]{1,0:T(8,128)S(1)}) custom-call(f32[1024,512]{1,0:T(8,128)S(1)} %turn_units.1.old_ref), custom_call_target="tpu_custom_call" | custom-call | tf_op jit(solution)/shard_map/exchange/pallas_call | solution.py:337
  284.4 77.0 %turn.1 = f32[1024,512]{1,0:T(8,128)} custom-call(f32[1280,128]{1,0:T(8,128)S(1)} %get-tuple-element.11.packed, f32[1024,512]{1,0:T(8,128)S(1)} %get-tuple-element.12.panel), custom_call_target="tpu_custom_call" | custom-call | tf_op jit(solution)/shard_map/turn/pallas_call | solution.py:462
Async XLA Ops:
  0.0 0.7 copy-start
  0.7 0.7 copy-start.1
  1.4 0.7 copy-start.3
  15.6 143.5 %copy-start.2 = (s32[1,8]{1,0:T(1,128)S(1)}, s32[1,8]{1,0:T(1,128)}, u32[]{:S(2)}) copy-start(s32[1,8]{1,0:T(1,128)} %counts_ref.3) | copy-start | bytes 100

commit v2 on v1

--- a/solution.py
+++ b/solution.py
@@ -13,7 +13,7 @@
 WIDTH = 2 * BLOCK
 TILE = 128
 ALIGN = 8
-MARGIN = 16
+BAND = 64
 CHUNKS = 4
 NEWTON_STEPS = 18
 SERIES_BOUND = 1e-6
@@ -37,8 +37,8 @@
     return mul(a[0], b[0]) + (mul(a[0], b[1]) + mul(a[1], b[0]))
 
 
-def dot_three(a, b):
-    return dot_halves(halves(a), halves(b))
+def dot_once(a, b):
+    return jnp.dot(a.astype(jnp.bfloat16), b.astype(jnp.bfloat16), preferred_element_type=jnp.float32)
 
 
 def add_gram(main, cross, block):
@@ -114,73 +114,67 @@
         copy.wait_send()
 
 
-def seat_kernel(pairs, seating_ref, counts_ref, unit_ref, scale_ref, out_ref):
-    mine = lax.axis_index("pairs")
-    start = jnp.int32(0)
-    for k in range(pairs):
-        start = start + jnp.where(k < mine, counts_ref[0, k], 0)
-    block = unit_ref[0, 0]
-    live = lax.broadcasted_iota(jnp.int32, block.shape, 0) < counts_ref[0, mine]
-    scaled = jnp.where(live, block * scale_ref[...], 0.0)
-    margin = jnp.zeros((out_ref.shape[1] - block.shape[0], BLOCK), jnp.float32)
-    out_ref[0] = pltpu.roll(jnp.concatenate([scaled, margin], axis=0), start & (ALIGN - 1), 0)
-
-
-def seat(pairs, unit_rows, channel_scale, seating, unit_counts):
-    capacity, columns = unit_rows.shape[2:]
-    room = capacity + MARGIN
-    return pl.pallas_call(
-        functools.partial(seat_kernel, pairs),
-        out_shape=jax.ShapeDtypeStruct((pairs, room, WIDTH), jnp.float32),
-        grid_spec=pltpu.PrefetchScalarGridSpec(
-            num_scalar_prefetch=2,
-            grid=(2 * pairs,),
-            in_specs=[
-                pl.BlockSpec((1, 1, capacity, BLOCK), lambda i, seating, counts: (0, 0, 0, seating[i])),
-                pl.BlockSpec((1, BLOCK), lambda i, seating, counts: (0, seating[i])),
-            ],
-            out_specs=pl.BlockSpec((1, room, BLOCK), lambda i, seating, counts: (i // 2, 0, i % 2)),
-        ),
-        compiler_params=pltpu.CompilerParams(vmem_limit_bytes=VMEM_LIMIT),
-        name="seat",
-    )(seating, unit_counts, unit_rows, channel_scale)
-
-
 def collect_kernel(
     pairs, rows, room,
-    seated, units_ref, gram_ref,
-    landed, main, cross, packed, parts, total,
-    send_sem, recv_sem, keep_sem, out_sem, scatter_send, scatter_recv, gather_send, gather_recv,
+    unit_ref, scale_ref, seating_ref, counts_ref, units_ref, gram_ref,
+    unit, seated, landed, main, cross, packed, parts, total,
+    send_sem, recv_sem, load_sem, out_sem, scatter_send, scatter_recv, gather_send, gather_recv,
 ):
     mine = lax.axis_index("pairs")
     barrier = pltpu.get_barrier_semaphore()
     signal_peers(barrier, "pairs", pairs)
     signal_peers(barrier, "rows", rows)
-    keep = pltpu.make_async_copy(seated.at[mine], landed.at[mine], keep_sem)
-    keep.start()
+    load = pltpu.make_async_copy(unit_ref.at[0, 0], unit, load_sem)
+    load.start()
     main[...] = jnp.zeros_like(main)
     cross[...] = jnp.zeros_like(cross)
+    band_row = lax.broadcasted_iota(jnp.int32, (BAND, BLOCK), 0)
+    own_count = counts_ref[0, mine]
+    load.wait()
     pl.semaphore_wait(barrier, pairs + rows - 2)
+
+    blocks = unit.shape[1] // BLOCK
+
+    def choose(ref, rows, seat):
+        chosen = ref[rows, pl.ds(0, BLOCK)]
+        at = jnp.broadcast_to(seat, chosen.shape)
+        for index in range(1, blocks):
+            chosen = jnp.where(at == index, ref[rows, pl.ds(index * BLOCK, BLOCK)], chosen)
+        return chosen
+
+    def fill(block, pair):
+        for h in range(2):
+            seat = seating_ref[2 * pair + h]
+            scale = choose(scale_ref, pl.ds(0, 1), seat)
+
+            def part(i, carry):
+                rows = pl.ds(pl.multiple_of(i * BAND, BAND), BAND)
+                live = band_row + i * BAND < own_count
+                block[rows, pl.ds(h * BLOCK, BLOCK)] = jnp.where(live, choose(unit, rows, seat) * scale, 0.0)
+                return carry
+
+            lax.fori_loop(0, room // BAND, part, 0)
 
     def copy_to(d):
         peer = lax.rem(mine + d, pairs)
-        return remote(seated.at[peer], landed.at[mine], send_sem.at[d - 1], recv_sem.at[d - 1], "pairs", peer)
+        return remote(seated.at[d - 1], landed.at[mine], send_sem.at[d - 1], recv_sem.at[d - 1], "pairs", peer)
 
     def write_out(source, d):
         return pltpu.make_async_copy(landed.at[source], units_ref.at[source], out_sem.at[d])
 
     def send(d, carry):
+        fill(seated.at[d - 1], lax.rem(mine + d, pairs))
         copy_to(d).start()
         return carry
 
     lax.fori_loop(1, pairs, send, 0)
-    keep.wait()
+    fill(landed.at[mine], mine)
     write_out(mine, 0).start()
     add_gram(main, cross, landed[mine])
 
     def receive(d, carry):
         source = lax.rem(mine + pairs - d, pairs)
-        remote(seated.at[source], landed.at[source], send_sem.at[d - 1], recv_sem.at[d - 1], "pairs", source).wait_recv()
+        remote(seated.at[d - 1], landed.at[source], send_sem.at[d - 1], recv_sem.at[d - 1], "pairs", source).wait_recv()
         write_out(source, d).start()
         add_gram(main, cross, landed[source])
         return carry
@@ -222,17 +216,21 @@
 )
 
 
-def collect(pairs, rows, seated):
+def collect(pairs, rows, unit_rows, channel_scale, seating, unit_counts):
+    capacity, columns = unit_rows.shape[2:]
+    units = (pairs, capacity, WIDTH)
     return pl.pallas_call(
-        functools.partial(collect_kernel, pairs, rows, seated.shape[1]),
+        functools.partial(collect_kernel, pairs, rows, capacity),
         out_shape=(
-            jax.ShapeDtypeStruct(seated.shape, jnp.float32),
+            jax.ShapeDtypeStruct(units, jnp.float32),
             jax.ShapeDtypeStruct((PACKED, TILE), jnp.float32),
         ),
-        in_specs=[ANY_SPEC],
+        in_specs=[ANY_SPEC, VMEM_SPEC, SMEM_SPEC, SMEM_SPEC],
         out_specs=(ANY_SPEC, VMEM_SPEC),
         scratch_shapes=[
-            pltpu.VMEM(seated.shape, jnp.float32),
+            pltpu.VMEM((capacity, columns), jnp.float32),
+            pltpu.VMEM((pairs - 1, capacity, WIDTH), jnp.float32),
+            pltpu.VMEM(units, jnp.float32),
             *gram_scratch(rows),
             pltpu.SemaphoreType.DMA((pairs - 1,)),
             pltpu.SemaphoreType.DMA((pairs - 1,)),
@@ -244,7 +242,7 @@
             collective_id=0, has_side_effects=True, vmem_limit_bytes=VMEM_LIMIT
         ),
         name="collect",
-    )(seated)
+    )(unit_rows, channel_scale, seating, unit_counts)
 
 
 def exchange_kernel(
@@ -360,12 +358,19 @@
     def compact():
         load.wait()
         start = jnp.int32(0)
-        head = lax.broadcasted_iota(jnp.int32, (ALIGN, WIDTH), 0)
+        groups = room // ALIGN
+        lane_row = lax.broadcasted_iota(jnp.int32, (groups + 1, ALIGN, WIDTH), 1)
         for k in range(pairs):
             first = pl.multiple_of(start & -ALIGN, ALIGN)
-            top = pl.ds(first, ALIGN)
-            panel[top, :] = jnp.where(head < (start & (ALIGN - 1)), panel[top, :], units[k, pl.ds(0, ALIGN), :])
-            panel[pl.ds(pl.multiple_of(first + ALIGN, ALIGN), room - ALIGN), :] = units[k, pl.ds(ALIGN, room - ALIGN), :]
+            shift = start & (ALIGN - 1)
+            turned = pltpu.roll(units[k].reshape(groups, ALIGN, WIDTH), shift, 1)
+            before = panel[pl.ds(first, ALIGN), :].reshape(1, ALIGN, WIDTH)
+            shifted = jnp.where(
+                lane_row < shift,
+                jnp.concatenate([before, turned], axis=0),
+                jnp.concatenate([turned, turned[-1:]], axis=0),
+            )
+            panel[pl.ds(first, room + ALIGN), :] = shifted.reshape(room + ALIGN, WIDTH)
             start = start + counts_ref[0, k]
 
     turn_panel(packed, panel, out, compact, *scratch)
@@ -394,16 +399,16 @@
     )
     t_halves = halves(tangent[...])
     square[...] = dot_halves(t_halves, t_halves)
-    m_halves = halves(square[...])
-    fourth = dot_halves(m_halves, m_halves)
+    m_high = square[...].astype(jnp.bfloat16)
+    fourth = dot_once(m_high, m_high)
     rest = jnp.sum(fourth * fourth)
     short = rest <= SERIES_BOUND
 
     @pl.when(short)
     def _():
         first = tangent[...] + square[...]
-        second = first + dot_halves(halves(first), m_halves)
-        change[...] = 2.0 * (second + dot_three(second, fourth))
+        second = first + dot_once(first, m_high)
+        change[...] = 2.0 * (second + dot_once(second, fourth))
 
     @pl.when(jnp.logical_not(short))
     def _():
@@ -449,7 +454,7 @@
         out_specs=VMEM_SPEC,
         scratch_shapes=[
             pltpu.VMEM(units.shape, jnp.float32),
-            pltpu.VMEM((ROWS_DEV + room, WIDTH), jnp.float32),
+            pltpu.VMEM((ROWS_DEV + room + ALIGN, WIDTH), jnp.float32),
             pltpu.SemaphoreType.DMA,
             *[pltpu.VMEM((WIDTH, WIDTH), jnp.float32)] * 4,
         ],
@@ -471,8 +476,7 @@
 
 
 def local(pairs, rows, unit_rows, unit_counts, seating, channel_scale):
-    seated = seat(pairs, unit_rows, channel_scale[None, :], seating, unit_counts)
-    units, gram = collect(pairs, rows, seated)
+    units, gram = collect(pairs, rows, unit_rows, channel_scale[None, :], seating, unit_counts)
     panel = turn_units(unit_counts, gram, units)
     for round_index in range(1, ROUNDS):
         panel, gram = exchange(pairs, rows, panel)

time: 362 us -> 342 us (0.945)
  Pallas kernels: 359 us -> 340 us
    pallas_call x2 -> x1, Pallas kernels: 157 us -> 141 us  [collect(): pl.pallas_call(functools.partial(collect_kernel, pairs, rows, capacity),...]
where the time goes in v2:
time: 342 us
  Pallas kernels  340 us (99%)
    pallas_call x1, Pallas kernels, collect(): pl.pallas_call(functools.partial(collect_kernel, pairs, rows, capacity),...  141 us
    pallas_call x1, Pallas kernels, turn(): pl.pallas_call(turn_kernel, out_shape=PANEL_AND_GRAM[0], in_specs=[VMEM_S...  76.4 us
    pallas_call x1, Pallas kernels, turn_units(): pl.pallas_call(turn_units_kernel, out_shape=PANEL_AND_GRAM[0], in_specs=[...  76.4 us
    pallas_call x1, Pallas kernels, exchange(): pl.pallas_call(functools.partial(exchange_kernel, pairs, rows), out_shape...  46.6 us

profile of v2, /device:TPU:16, one launch (start us, length us, event | category | flops | bytes accessed | tf_op | source)
XLA Modules:
  0.0 341.9 jit_solution(7068092827678947000)
XLA Ops:
  0.0 0.0 copy-start
  0.0 0.7 copy-done
  0.7 0.0 copy-start.1
  0.7 0.7 copy-done.1
  1.4 0.0 copy-start.2
  1.4 0.7 copy-done.2
  2.0 140.5 %collect.1 = (f32[8,384,512]{2,1,0:T(8,128)}, f32[1280,128]{1,0:T(8,128)S(1)}) custom-call(f32[1,1,384,4096]{3,2,1,0:T(8,128)} %unit_ref.1, f32[1,4096]{1,0:T(1,128)S(1)} %bitcast.1, s32[16]{0:T(128)S(1)} %copy-done.2, s32[1,8]{1,0:T(1,128)S(1)} %copy-done.1), custom_call_target="tpu_custom_call" | custom-call | tf_op jit(solution)/shard_map/collect/pallas_call | solution.py:222
  142.6 76.4 %turn_units.1.old_ref = f32[1024,512]{1,0:T(8,128)S(1)} custom-call(s32[1,8]{1,0:T(1,128)S(1)} %copy-done.1, f32[1280,128]{1,0:T(8,128)S(1)} %get-tuple-element.9.packed, f32[8,384,512]{2,1,0:T(8,128)} %get-tuple-element.10.units_ref), custom_call_target="tpu_custom_call" | custom-call | tf_op jit(solution)/shard_map/turn_units/pallas_call | solution.py:450
  218.9 46.6 %exchange.1 = (f32[1024,512]{1,0:T(8,128)S(1)}, f32[1280,128]{1,0:T(8,128)S(1)}) custom-call(f32[1024,512]{1,0:T(8,128)S(1)} %turn_units.1.old_ref), custom_call_target="tpu_custom_call" | custom-call | tf_op jit(solution)/shard_map/exchange/pallas_call | solution.py:335
  265.5 76.4 %turn.1 = f32[1024,512]{1,0:T(8,128)} custom-call(f32[1280,128]{1,0:T(8,128)S(1)} %get-tuple-element.11.packed, f32[1024,512]{1,0:T(8,128)S(1)} %get-tuple-element.12.panel), custom_call_target="tpu_custom_call" | custom-call | tf_op jit(solution)/shard_map/turn/pallas_call | solution.py:467
Async XLA Ops:
  0.0 0.7 copy-start
  0.7 0.7 copy-start.1
  1.4 0.7 copy-start.2

commit v3 on v2

--- a/solution.py
+++ b/solution.py
@@ -22,8 +22,12 @@
 epsilon = 1e-06
 
 MESH = pl.DeviceIdType.MESH
-TILE_PAIRS = [(i, j) for i in range(WIDTH // TILE) for j in range(i, WIDTH // TILE)]
-PACKED = len(TILE_PAIRS) * TILE
+TILES = WIDTH // TILE
+OFF_DIAGONAL = [(i, j) for i in range(TILES) for j in range(i + 1, TILES)]
+DIAGONAL_AT = len(OFF_DIAGONAL) * TILE
+EXTRA_AT = DIAGONAL_AT + TILES // 2 * TILE
+EXTRA = 64
+PACKED = EXTRA_AT + EXTRA
 
 
 def halves(x):
@@ -52,12 +56,45 @@
     cross[...] += mul(high, low)
 
 
+def tile_iotas():
+    shape = (TILE, TILE)
+    return lax.broadcasted_iota(jnp.int32, shape, 0), lax.broadcasted_iota(jnp.int32, shape, 1)
+
+
 def pack_gram(main, cross, packed):
-    for t, (i, j) in enumerate(TILE_PAIRS):
+    def tile(i, j):
         rows, cols = pl.ds(i * TILE, TILE), pl.ds(j * TILE, TILE)
-        packed[pl.ds(t * TILE, TILE), :] = (
-            main[rows, cols] + cross[rows, cols] + cross[cols, rows].T
-        )
+        return main[rows, cols] + cross[rows, cols] + cross[cols, rows].T
+
+    row, col = tile_iotas()
+    for t, (i, j) in enumerate(OFF_DIAGONAL):
+        packed[pl.ds(t * TILE, TILE), :] = tile(i, j)
+    packed[pl.ds(EXTRA_AT, EXTRA), :] = jnp.zeros((EXTRA, TILE), jnp.float32)
+    for t in range(TILES // 2):
+        lower = tile(2 * t + 1, 2 * t + 1)
+        packed[pl.ds(DIAGONAL_AT + t * TILE, TILE), :] = jnp.where(row <= col, tile(2 * t, 2 * t), lower)
+        packed[pl.ds(EXTRA_AT + t, 1), :] = jnp.sum(jnp.where(row == col, lower, 0.0), axis=0, keepdims=True)
+
+
+def unpack_gram(packed, gram):
+    row, col = tile_iotas()
+    across, along = [], []
+    for t, (i, j) in enumerate(OFF_DIAGONAL):
+        tile = packed[pl.ds(t * TILE, TILE), :]
+        gram[pl.ds(i * TILE, TILE), pl.ds(j * TILE, TILE)] = tile
+        gram[pl.ds(j * TILE, TILE), pl.ds(i * TILE, TILE)] = tile.T
+    for t in range(TILES // 2):
+        both = packed[pl.ds(DIAGONAL_AT + t * TILE, TILE), :]
+        flipped = both.T
+        upper = jnp.where(row <= col, both, flipped)
+        lower = jnp.where(row > col, both, flipped)
+        lower = jnp.where(row == col, packed[pl.ds(EXTRA_AT + t, 1), :], lower)
+        for i, tile in ((2 * t, upper), (2 * t + 1, lower)):
+            gram[pl.ds(i * TILE, TILE), pl.ds(i * TILE, TILE)] = tile
+            kept = jnp.where(row == col, tile, 0.0)
+            across.append(jnp.sum(kept, axis=0, keepdims=True))
+            along.append(jnp.sum(kept, axis=1, keepdims=True))
+    return jnp.concatenate(across, axis=1), jnp.concatenate(along, axis=0)
 
 
 def remote(src, dst, send_sem, recv_sem, axis, index):
@@ -114,6 +151,38 @@
         copy.wait_send()
 
 
+def send_orders(pairs):
+    if pairs != 8:
+        return [[(me + d) % pairs for d in range(1, pairs)] for me in range(pairs)]
+    orders = []
+    for me in range(pairs):
+        flips = [6, 7, 4, 5, 1, 2, 3] if 2 <= me < 6 else [2, 3, 1, 4, 5, 6, 7]
+        orders.append([me ^ flip for flip in flips])
+    return orders
+
+
+def receive_orders(pairs):
+    if pairs != 8:
+        return [[(me + pairs - d) % pairs for d in range(1, pairs)] for me in range(pairs)]
+    inner, outer = [2, 4, 5, 6, 7, 8, 9], [0, 1, 3, 10, 11, 12, 13]
+    sends = send_orders(pairs)
+
+    def due(source, me):
+        return (inner if 2 <= source < 6 else outer)[sends[source].index(me)]
+
+    return [
+        sorted([source for source in range(pairs) if source != me], key=lambda source: due(source, me))
+        for me in range(pairs)
+    ]
+
+
+def pick(orders, mine, step):
+    chosen = jnp.int32(orders[0][step])
+    for me in range(1, len(orders)):
+        chosen = jnp.where(mine == me, jnp.int32(orders[me][step]), chosen)
+    return chosen
+
+
 def collect_kernel(
     pairs, rows, room,
     unit_ref, scale_ref, seating_ref, counts_ref, units_ref, gram_ref,
@@ -121,6 +190,7 @@
     send_sem, recv_sem, load_sem, out_sem, scatter_send, scatter_recv, gather_send, gather_recv,
 ):
     mine = lax.axis_index("pairs")
+    to, from_ = send_orders(pairs), receive_orders(pairs)
     barrier = pltpu.get_barrier_semaphore()
     signal_peers(barrier, "pairs", pairs)
     signal_peers(barrier, "rows", rows)
@@ -155,42 +225,31 @@
 
             lax.fori_loop(0, room // BAND, part, 0)
 
-    def copy_to(d):
-        peer = lax.rem(mine + d, pairs)
-        return remote(seated.at[d - 1], landed.at[mine], send_sem.at[d - 1], recv_sem.at[d - 1], "pairs", peer)
-
-    def write_out(source, d):
-        return pltpu.make_async_copy(landed.at[source], units_ref.at[source], out_sem.at[d])
-
-    def send(d, carry):
-        fill(seated.at[d - 1], lax.rem(mine + d, pairs))
-        copy_to(d).start()
-        return carry
-
-    lax.fori_loop(1, pairs, send, 0)
+    def write_out(source):
+        return pltpu.make_async_copy(landed.at[source], units_ref.at[source], out_sem.at[source])
+
+    sends = []
+    for step in range(pairs - 1):
+        peer = pick(to, mine, step)
+        fill(seated.at[step], peer)
+        copy = remote(seated.at[step], landed.at[mine], send_sem.at[step], recv_sem.at[mine], "pairs", peer)
+        copy.start()
+        sends.append(copy)
     fill(landed.at[mine], mine)
-    write_out(mine, 0).start()
+    write_out(mine).start()
     add_gram(main, cross, landed[mine])
-
-    def receive(d, carry):
-        source = lax.rem(mine + pairs - d, pairs)
-        remote(seated.at[d - 1], landed.at[source], send_sem.at[d - 1], recv_sem.at[d - 1], "pairs", source).wait_recv()
-        write_out(source, d).start()
+    sources = [pick(from_, mine, step) for step in range(pairs - 1)]
+    for source in sources:
+        remote(seated.at[0], landed.at[source], send_sem.at[0], recv_sem.at[source], "pairs", source).wait_recv()
+        write_out(source).start()
         add_gram(main, cross, landed[source])
-        return carry
-
-    lax.fori_loop(1, pairs, receive, 0)
     pack_gram(main, cross, packed)
     sum_over_rows(rows, packed, parts, total, scatter_send, scatter_recv, gather_send, gather_recv, lambda: None)
     gram_ref[...] = total[...]
-    write_out(mine, 0).wait()
-
-    def finish(d, carry):
-        copy_to(d).wait_send()
-        write_out(lax.rem(mine + pairs - d, pairs), d).wait()
-        return carry
-
-    lax.fori_loop(1, pairs, finish, 0)
+    for source in [mine, *sources]:
+        write_out(source).wait()
+    for copy in sends:
+        copy.wait_send()
 
 
 def gram_scratch(rows):
@@ -233,7 +292,7 @@
             pltpu.VMEM(units, jnp.float32),
             *gram_scratch(rows),
             pltpu.SemaphoreType.DMA((pairs - 1,)),
-            pltpu.SemaphoreType.DMA((pairs - 1,)),
+            pltpu.SemaphoreType.DMA((pairs,)),
             pltpu.SemaphoreType.DMA,
             pltpu.SemaphoreType.DMA((pairs,)),
             *row_sems(rows),
@@ -381,19 +440,7 @@
 
 
 def turn_panel(packed, panel, out, prepare, gram, tangent, square, change):
-    on_diag = lax.broadcasted_iota(jnp.int32, (TILE, TILE), 0) == lax.broadcasted_iota(jnp.int32, (TILE, TILE), 1)
-    across, along = [], []
-    for t, (i, j) in enumerate(TILE_PAIRS):
-        tile = packed[pl.ds(t * TILE, TILE), :]
-        gram[pl.ds(i * TILE, TILE), pl.ds(j * TILE, TILE)] = tile
-        if i == j:
-            kept = jnp.where(on_diag, tile, 0.0)
-            across.append(jnp.sum(kept, axis=0, keepdims=True))
-            along.append(jnp.sum(kept, axis=1, keepdims=True))
-        else:
-            gram[pl.ds(j * TILE, TILE), pl.ds(i * TILE, TILE)] = tile.T
-    diag_row = jnp.concatenate(across, axis=1)
-    diag_col = jnp.concatenate(along, axis=0)
+    diag_row, diag_col = unpack_gram(packed, gram)
     tangent[...] = 0.5 * (
         gram[...] * (diag_row - diag_col) / (2.0 * (diag_col**2 + diag_row**2) + epsilon)
     )

time: 342 us -> 345 us (level)
  the two profiles are of different devices: /device:TPU:16 before, /device:TPU:8 now
where the time goes in v3:
time: 345 us; the launch traced here: 344 us
  Pallas kernels  342 us (99%)
    pallas_call x1, Pallas kernels, collect(): pl.pallas_call(functools.partial(collect_kernel, pairs, rows, capacity),...  140 us
    pallas_call x1, Pallas kernels, turn(): pl.pallas_call(turn_kernel, out_shape=PANEL_AND_GRAM[0], in_specs=[VMEM_S...  76.8 us
    pallas_call x1, Pallas kernels, turn_units(): pl.pallas_call(turn_units_kernel, out_shape=PANEL_AND_GRAM[0], in_specs=[...  76.7 us
    pallas_call x1, Pallas kernels, exchange(): pl.pallas_call(functools.partial(exchange_kernel, pairs, rows), out_shape...  49.3 us

profile of v3, /device:TPU:8, one launch (start us, length us, event | category | flops | bytes accessed | tf_op | source)
XLA Modules:
  0.0 344.4 jit_solution(7025365231089760623)
XLA Ops:
  0.0 0.0 copy-start
  0.0 0.7 copy-done
  0.7 0.0 copy-start.1
  0.7 0.7 copy-done.1
  1.4 0.0 copy-start.2
  1.4 0.7 copy-done.2
  2.0 139.5 %collect.1 = (f32[8,384,512]{2,1,0:T(8,128)}, f32[1088,128]{1,0:T(8,128)S(1)}) custom-call(f32[1,1,384,4096]{3,2,1,0:T(8,128)} %unit_ref.1, f32[1,4096]{1,0:T(1,128)S(1)} %bitcast.1, s32[16]{0:T(128)S(1)} %copy-done.2, s32[1,8]{1,0:T(1,128)S(1)} %copy-done.1), custom_call_target="tpu_custom_call" | custom-call | tf_op jit(solution)/shard_map/collect/pallas_call | solution.py:281
  141.6 76.7 %turn_units.1.old_ref = f32[1024,512]{1,0:T(8,128)S(1)} custom-call(s32[1,8]{1,0:T(1,128)S(1)} %copy-done.1, f32[1088,128]{1,0:T(8,128)S(1)} %get-tuple-element.9.packed, f32[8,384,512]{2,1,0:T(8,128)} %get-tuple-element.10.units_ref), custom_call_target="tpu_custom_call" | custom-call | tf_op jit(solution)/shard_map/turn_units/pallas_call | solution.py:497
  218.3 49.3 %exchange.1 = (f32[1024,512]{1,0:T(8,128)S(1)}, f32[1088,128]{1,0:T(8,128)S(1)}) custom-call(f32[1024,512]{1,0:T(8,128)S(1)} %turn_units.1.old_ref), custom_call_target="tpu_custom_call" | custom-call | tf_op jit(solution)/shard_map/exchange/pallas_call | solution.py:394
  267.6 76.8 %turn.1 = f32[1024,512]{1,0:T(8,128)} custom-call(f32[1088,128]{1,0:T(8,128)S(1)} %get-tuple-element.11.packed, f32[1024,512]{1,0:T(8,128)S(1)} %get-tuple-element.12.panel), custom_call_target="tpu_custom_call" | custom-call | tf_op jit(solution)/shard_map/turn/pallas_call | solution.py:514
Async XLA Ops:
  0.0 0.7 copy-start
  0.7 0.7 copy-start.1
  1.4 0.7 copy-start.2

commit v4 on v3

--- a/solution.py
+++ b/solution.py
@@ -151,38 +151,6 @@
         copy.wait_send()
 
 
-def send_orders(pairs):
-    if pairs != 8:
-        return [[(me + d) % pairs for d in range(1, pairs)] for me in range(pairs)]
-    orders = []
-    for me in range(pairs):
-        flips = [6, 7, 4, 5, 1, 2, 3] if 2 <= me < 6 else [2, 3, 1, 4, 5, 6, 7]
-        orders.append([me ^ flip for flip in flips])
-    return orders
-
-
-def receive_orders(pairs):
-    if pairs != 8:
-        return [[(me + pairs - d) % pairs for d in range(1, pairs)] for me in range(pairs)]
-    inner, outer = [2, 4, 5, 6, 7, 8, 9], [0, 1, 3, 10, 11, 12, 13]
-    sends = send_orders(pairs)
-
-    def due(source, me):
-        return (inner if 2 <= source < 6 else outer)[sends[source].index(me)]
-
-    return [
-        sorted([source for source in range(pairs) if source != me], key=lambda source: due(source, me))
-        for me in range(pairs)
-    ]
-
-
-def pick(orders, mine, step):
-    chosen = jnp.int32(orders[0][step])
-    for me in range(1, len(orders)):
-        chosen = jnp.where(mine == me, jnp.int32(orders[me][step]), chosen)
-    return chosen
-
-
 def collect_kernel(
     pairs, rows, room,
     unit_ref, scale_ref, seating_ref, counts_ref, units_ref, gram_ref,
@@ -190,7 +158,6 @@
     send_sem, recv_sem, load_sem, out_sem, scatter_send, scatter_recv, gather_send, gather_recv,
 ):
     mine = lax.axis_index("pairs")
-    to, from_ = send_orders(pairs), receive_orders(pairs)
     barrier = pltpu.get_barrier_semaphore()
     signal_peers(barrier, "pairs", pairs)
     signal_peers(barrier, "rows", rows)
@@ -230,7 +197,7 @@
 
     sends = []
     for step in range(pairs - 1):
-        peer = pick(to, mine, step)
+        peer = lax.rem(mine + step + 1, pairs)
         fill(seated.at[step], peer)
         copy = remote(seated.at[step], landed.at[mine], send_sem.at[step], recv_sem.at[mine], "pairs", peer)
         copy.start()
@@ -238,7 +205,7 @@
     fill(landed.at[mine], mine)
     write_out(mine).start()
     add_gram(main, cross, landed[mine])
-    sources = [pick(from_, mine, step) for step in range(pairs - 1)]
+    sources = [lax.rem(mine + pairs - d, pairs) for d in range(1, pairs)]
     for source in sources:
         remote(seated.at[0], landed.at[source], send_sem.at[0], recv_sem.at[source], "pairs", source).wait_recv()
         write_out(source).start()

time: 345 us -> 339 us (0.983)
  the two profiles are of different devices: /device:TPU:8 before, /device:TPU:16 now
where the time goes in v4:
time: 339 us
  Pallas kernels  336 us (99%)
    pallas_call x1, Pallas kernels, collect(): pl.pallas_call(functools.partial(collect_kernel, pairs, rows, capacity),...  141 us
    pallas_call x1, Pallas kernels, turn(): pl.pallas_call(turn_kernel, out_shape=PANEL_AND_GRAM[0], in_specs=[VMEM_S...  76.8 us
    pallas_call x1, Pallas kernels, turn_units(): pl.pallas_call(turn_units_kernel, out_shape=PANEL_AND_GRAM[0], in_specs=[...  76.7 us
    pallas_call x1, Pallas kernels, exchange(): pl.pallas_call(functools.partial(exchange_kernel, pairs, rows), out_shape...  42.5 us

profile of v4, /device:TPU:16, one launch (start us, length us, event | category | flops | bytes accessed | tf_op | source)
XLA Modules:
  0.0 338.5 jit_solution(15256849717771175322)
XLA Ops:
  0.0 0.0 copy-start
  0.0 0.7 copy-done
  0.7 0.0 copy-start.1
  0.7 0.7 copy-done.1
  1.4 0.0 copy-start.2
  1.4 0.7 copy-done.2
  2.0 140.5 %collect.1 = (f32[8,384,512]{2,1,0:T(8,128)}, f32[1088,128]{1,0:T(8,128)S(1)}) custom-call(f32[1,1,384,4096]{3,2,1,0:T(8,128)} %unit_ref.1, f32[1,4096]{1,0:T(1,128)S(1)} %bitcast.1, s32[16]{0:T(128)S(1)} %copy-done.2, s32[1,8]{1,0:T(1,128)S(1)} %copy-done.1), custom_call_target="tpu_custom_call" | custom-call | tf_op jit(solution)/shard_map/collect/pallas_call | solution.py:248
  142.6 76.7 %turn_units.1.old_ref = f32[1024,512]{1,0:T(8,128)S(1)} custom-call(s32[1,8]{1,0:T(1,128)S(1)} %copy-done.1, f32[1088,128]{1,0:T(8,128)S(1)} %get-tuple-element.9.packed, f32[8,384,512]{2,1,0:T(8,128)} %get-tuple-element.10.units_ref), custom_call_target="tpu_custom_call" | custom-call | tf_op jit(solution)/shard_map/turn_units/pallas_call | solution.py:464
  219.3 42.5 %exchange.1 = (f32[1024,512]{1,0:T(8,128)S(1)}, f32[1088,128]{1,0:T(8,128)S(1)}) custom-call(f32[1024,512]{1,0:T(8,128)S(1)} %turn_units.1.old_ref), custom_call_target="tpu_custom_call" | custom-call | tf_op jit(solution)/shard_map/exchange/pallas_call | solution.py:361
  261.7 76.8 %turn.1 = f32[1024,512]{1,0:T(8,128)} custom-call(f32[1088,128]{1,0:T(8,128)S(1)} %get-tuple-element.11.packed, f32[1024,512]{1,0:T(8,128)S(1)} %get-tuple-element.12.panel), custom_call_target="tpu_custom_call" | custom-call | tf_op jit(solution)/shard_map/turn/pallas_call | solution.py:481
Async XLA Ops:
  0.0 0.7 copy-start
  0.7 0.7 copy-start.1
  1.4 0.7 copy-start.2

commit v5 on v4

--- a/solution.py
+++ b/solution.py
@@ -196,8 +196,9 @@
         return pltpu.make_async_copy(landed.at[source], units_ref.at[source], out_sem.at[source])
 
     sends = []
-    for step in range(pairs - 1):
-        peer = lax.rem(mine + step + 1, pairs)
+    farthest_first = sorted(range(1, pairs), key=lambda d: abs(d - pairs // 2))
+    for step, d in enumerate(farthest_first):
+        peer = lax.rem(mine + d, pairs)
         fill(seated.at[step], peer)
         copy = remote(seated.at[step], landed.at[mine], send_sem.at[step], recv_sem.at[mine], "pairs", peer)
         copy.start()
@@ -205,7 +206,7 @@
     fill(landed.at[mine], mine)
     write_out(mine).start()
     add_gram(main, cross, landed[mine])
-    sources = [lax.rem(mine + pairs - d, pairs) for d in range(1, pairs)]
+    sources = [lax.rem(mine + pairs - d, pairs) for d in farthest_first]
     for source in sources:
         remote(seated.at[0], landed.at[source], send_sem.at[0], recv_sem.at[source], "pairs", source).wait_recv()
         write_out(source).start()

time: 339 us -> 338 us (level)
    pallas_call x1, Pallas kernels: 42.5 us -> 26.3 us  [exchange(): pl.pallas_call(functools.partial(exchange_kernel, pairs, rows), out_shape...]
    pallas_call x1, Pallas kernels: 141 us -> 155 us  [collect(): pl.pallas_call(functools.partial(collect_kernel, pairs, rows, capacity),...]
where the time goes in v5:
time: 338 us; the launch traced here: 337 us
  Pallas kernels  335 us (99%)
    pallas_call x1, Pallas kernels, collect(): pl.pallas_call(functools.partial(collect_kernel, pairs, rows, capacity),...  155 us
    pallas_call x1, Pallas kernels, turn(): pl.pallas_call(turn_kernel, out_shape=PANEL_AND_GRAM[0], in_specs=[VMEM_S...  76.8 us
    pallas_call x1, Pallas kernels, turn_units(): pl.pallas_call(turn_units_kernel, out_shape=PANEL_AND_GRAM[0], in_specs=[...  76.7 us
    pallas_call x1, Pallas kernels, exchange(): pl.pallas_call(functools.partial(exchange_kernel, pairs, rows), out_shape...  26.3 us

profile of v5, /device:TPU:16, one launch (start us, length us, event | category | flops | bytes accessed | tf_op | source)
XLA Modules:
  0.0 337.3 jit_solution(16713473739885858222)
XLA Ops:
  0.0 0.0 copy-start
  0.0 0.7 copy-done
  0.7 0.0 copy-start.1
  0.7 0.7 copy-done.1
  1.4 0.0 copy-start.2
  1.4 0.7 copy-done.2
  2.0 155.4 %collect.1 = (f32[8,384,512]{2,1,0:T(8,128)}, f32[1088,128]{1,0:T(8,128)S(1)}) custom-call(f32[1,1,384,4096]{3,2,1,0:T(8,128)} %unit_ref.1, f32[1,4096]{1,0:T(1,128)S(1)} %bitcast.1, s32[16]{0:T(128)S(1)} %copy-done.2, s32[1,8]{1,0:T(1,128)S(1)} %copy-done.1), custom_call_target="tpu_custom_call" | custom-call | tf_op jit(solution)/shard_map/collect/pallas_call | solution.py:249
  157.5 76.7 %turn_units.1.old_ref = f32[1024,512]{1,0:T(8,128)S(1)} custom-call(s32[1,8]{1,0:T(1,128)S(1)} %copy-done.1, f32[1088,128]{1,0:T(8,128)S(1)} %get-tuple-element.9.packed, f32[8,384,512]{2,1,0:T(8,128)} %get-tuple-element.10.units_ref), custom_call_target="tpu_custom_call" | custom-call | tf_op jit(solution)/shard_map/turn_units/pallas_call | solution.py:465
  234.1 26.3 %exchange.1 = (f32[1024,512]{1,0:T(8,128)S(1)}, f32[1088,128]{1,0:T(8,128)S(1)}) custom-call(f32[1024,512]{1,0:T(8,128)S(1)} %turn_units.1.old_ref), custom_call_target="tpu_custom_call" | custom-call | tf_op jit(solution)/shard_map/exchange/pallas_call | solution.py:362
  260.5 76.8 %turn.1 = f32[1024,512]{1,0:T(8,128)} custom-call(f32[1088,128]{1,0:T(8,128)S(1)} %get-tuple-element.11.packed, f32[1024,512]{1,0:T(8,128)S(1)} %get-tuple-element.12.panel), custom_call_target="tpu_custom_call" | custom-call | tf_op jit(solution)/shard_map/turn/pallas_call | solution.py:482
Async XLA Ops:
  0.0 0.7 copy-start
  0.7 0.7 copy-start.1
  1.4 0.7 copy-start.2
